TPU v7x, 512 devices: a whole 4x8x8 slice. The times are simulated.
512 devices in a mesh: stu: 32 (over y, z_lo, core), item: 16 (over z_hi, x).
Axes of the slice: x: 4, y: 8, z: 8 (z_hi: 4, z_lo: 2; z = z_hi * 2 + z_lo), core: 2. Of those that a mesh axis runs over, the one named last changes fastest.
Arguments:
- attempts: bfloat16 [65536, 12288], P('stu', 'item'), may hold values from -0.5 to 0.5
- item_factor: bfloat16 [12288, 64], P('item'), may hold values from -0.0546875 to 0.0546875
- core_factor: float32 [64, 64], replicated, may hold values from -1 to 1.5
- student_weights: float32 [128, 64], P('stu'), may hold values from 0.3 to 3
- blocks: int32 [32, 4], P('stu'), may hold values from 1 to 8, 16 in all within a row
Outputs:
- item_mttkrp: float32 [12288, 64], P('item')
- shared_mttkrp: float32 [64, 64], replicated
- student_mttkrp: float32 [128, 64], P('stu')
Inputs may be any that keep to these rules, and one draw needn't show every extreme that they name: Each row of blocks sums to 16, and some student of each row has exactly 8 blocks.
All inputs are finite; a program needn't handle non-finite values.
Results may differ from a plain program's by a relative error of at most 0.0003.
Values sent between devices are 32-bit elements; how exact they have to be, the bound alone decides.
No kernel may reach another device: no remote copies, remote signals or barrier semaphores. Data moves between devices by JAX's collectives and lax.ppermute only.
A program may use at most 64 MiB of HBM per device.

v0:
```python
import jax
import jax.numpy as jnp
from jax import lax
from jax.sharding import PartitionSpec as P

NS_STEPS = 6
HIGHEST = lax.Precision.HIGHEST


def owner_table(counts, row_total, group_rows):
    end_rows = jnp.cumsum(counts) * 128
    start_rows = end_rows - counts * 128
    places = jnp.arange(row_total // group_rows, dtype=jnp.int32) * group_rows
    inside = (places[:, None] >= start_rows[None, :]) & (places[:, None] < end_rows[None, :])
    return inside.astype(jnp.float32)


def polar_factor(target, owners, group_rows, combine):
    row_total, width = target.shape
    blocked = target.reshape(row_total // group_rows, group_rows, width)
    identity = jnp.eye(width, dtype=jnp.float32)

    def student_gram(blocked_now):
        grams = jnp.einsum("gla,glb->gab", blocked_now, blocked_now, precision=HIGHEST)
        return combine(jnp.einsum("gk,gab->kab", owners, grams, precision=HIGHEST))

    gram_now = student_gram(blocked)
    diagonal_sum = jnp.sum(gram_now * identity, axis=(1, 2))
    inverse_norm = 1.0 / jnp.sqrt(diagonal_sum + 1e-06)
    blocked = blocked * jnp.dot(owners, inverse_norm, precision=HIGHEST)[:, None, None]
    gram_now = gram_now * (inverse_norm * inverse_norm)[:, None, None]
    for iteration in range(NS_STEPS):
        if iteration > 0:
            gram_now = student_gram(blocked)
        factor = 1.5 * identity - 0.5 * gram_now
        spread = jnp.einsum("gk,kab->gab", owners, factor, precision=HIGHEST)
        blocked = jnp.einsum("gla,gab->glb", blocked, spread, precision=HIGHEST)
    return blocked.reshape(row_total, width)


def student_cross(orthogonal, raw_sums, owners, group_rows):
    row_total, width = raw_sums.shape
    left_side = orthogonal.reshape(row_total // group_rows, group_rows, width)
    right_side = raw_sums.reshape(row_total // group_rows, group_rows, width)
    grams = jnp.einsum("gla,glb->gab", left_side, right_side, precision=HIGHEST)
    return jnp.einsum("gk,gab->kab", owners, grams, precision=HIGHEST)


def scaled_target(raw_sums, owners, group_rows, weights_here, core_factor):
    row_total, width = raw_sums.shape
    row_scale = jnp.dot(owners, weights_here, precision=HIGHEST)
    scaled = raw_sums.reshape(row_total // group_rows, group_rows, width) * row_scale[:, None, :]
    return jnp.dot(scaled.reshape(row_total, width), core_factor.T, precision=HIGHEST)


def local(attempts, item_factor, core_factor, student_weights, blocks):
    row_total = attempts.shape[0]
    width = item_factor.shape[1]
    counts = blocks[0]
    full_owners = owner_table(counts, row_total, 128)
    local_sums = jnp.dot(attempts, item_factor, preferred_element_type=jnp.float32)
    raw_sums = lax.psum(local_sums, "item")
    target = scaled_target(raw_sums, full_owners, 128, student_weights, core_factor)
    orthogonal = polar_factor(target, full_owners, 128, lambda summand: summand)
    crossed = student_cross(orthogonal, raw_sums, full_owners, 128)
    row_scale = jnp.dot(full_owners, student_weights, precision=HIGHEST)
    lifted = jnp.dot(orthogonal, core_factor, precision=HIGHEST)
    lifted = lifted.reshape(row_total // 128, 128, width) * row_scale[:, None, :]
    weighted = lifted.reshape(row_total, width).astype(jnp.bfloat16)
    item_part = lax.dot_general(
        attempts, weighted, (((0,), (0,)), ((), ())), preferred_element_type=jnp.float32
    )
    shared_part = jnp.einsum("kab,kb->ab", crossed, student_weights, precision=HIGHEST)
    student_part = jnp.einsum("ab,kab->kb", core_factor, crossed, precision=HIGHEST)
    item_total, shared_total = lax.psum((item_part, shared_part), "stu")
    return (item_total, shared_total, student_part)


def solution(mesh):
    in_specs = (P("stu", "item"), P("item", None), P(), P("stu", None), P("stu", None))
    out_specs = (P("item", None), P(), P("stu", None))
    return jax.shard_map(local, mesh=mesh, in_specs=in_specs, out_specs=out_specs, check_vma=False)
```

profile of v0, /device:TPU:2, one launch (start us, length us, event | category | flops | bytes accessed | tf_op | source)
XLA Modules:
  0.0 437.9 jit_solution(16412960263734139279)
XLA Ops:
  7.2 0.0 copy-start
  7.2 0.0 copy-start.4
  7.2 0.0 copy-start.3
  7.2 0.0 copy-start.2
  7.2 0.0 all-reduce.3.cloned.1.call-start
  7.3 1.8 copy-done
  9.1 2.8 fusion.73
  11.8 0.0 all-reduce.3.cloned.1.call-update
  11.9 0.0 all-reduce.5.cloned.1.call-start
  11.9 0.0 copy-done.4
  11.9 0.2 reduce-window.4
  12.1 0.1 compare_and_fusion
  12.2 0.0 copy-done.3
  12.2 0.2 fusion.74
  12.4 0.1 copy.43
  12.5 176.2 %all-reduce.3.cloned.1.call-done = f32[2048,64]{0,1:T(8,128)} async-done(((f32[2048,64]{0,1:T(8,128)}), f32[2048,64]{0,1:T(8,128)}) %all-reduce.3.cloned.1.call-update) | async-done | bytes 524304 | tf_op jit(solution)/shard_map/psum | solution.py:62
  188.7 0.2 mul.120.clone
  188.9 0.0 copy-done.2
  188.9 1.8 fusion.11
  190.8 0.9 fusion.75
  191.7 0.8 multiply_reduce_fusion.2
  192.5 0.1 convolution_bitcast_fusion.1
  192.6 0.5 fusion.39
  193.1 1.1 fusion.31
  194.2 0.9 fusion.76
  195.2 0.6 fusion.6
  195.8 0.5 fusion.63
  196.3 1.1 fusion.28
  197.4 0.9 fusion.77
  198.3 0.6 fusion.5
  198.9 0.5 fusion.60
  199.4 1.1 fusion.25
  200.5 0.9 fusion.78
  201.4 0.6 fusion.4
  202.0 0.5 fusion.57
  202.5 1.3 fusion.22
  203.8 0.9 fusion.79
  204.7 0.6 fusion.3
  205.3 0.5 fusion.54
  205.8 1.1 fusion.19
  206.9 0.9 fusion.80
  207.8 0.6 fusion.2
  208.5 0.5 fusion.51
  208.9 1.1 fusion.16
  210.0 0.0 copy-start.1
  210.0 0.8 copy-done.1
  210.8 0.6 fusion.1
  211.4 1.3 convolution_bitcast_fusion
  212.8 0.0 all-reduce.5.cloned.1.call-update
  212.8 2.1 fusion.8
  215.0 0.7 multiply_reduce_fusion.1
  215.6 104.4 %psum.23 = f32[64,64]{1,0:T(8,128)} all-reduce(f32[64,64]{1,0:T(8,128)S(1)} %bitcast.121), channel_id=1, replica_groups=mesh['stu'=32,'item'=16] {'stu'}, use_global_device_ids=true, to_apply=%region_4.5 | all-reduce | flops 4096 | bytes 32768 | tf_op jit(solution)/shard_map/psum | solution.py:75
  320.1 0.7 multiply_reduce_fusion
  320.7 108.8 %all-reduce.5.cloned.1.call-done = f32[768,64]{0,1:T(8,128)} async-done(((f32[768,64]{0,1:T(8,128)}), f32[768,64]{0,1:T(8,128)}) %all-reduce.5.cloned.1.call-update) | async-done | bytes 196624 | tf_op jit(solution)/shard_map/psum | solution.py:75
  429.5 1.6 copy.97
  (6 shorter events, 0.0 us)
Async XLA Ops:
  7.2 1.9 copy-start
  7.2 4.7 %copy-start.4 = (s32[1,4]{1,0:T(1,128)S(1)}, s32[1,4]{1,0:T(1,128)}, u32[]{:S(2)}) copy-start(s32[1,4]{1,0:T(1,128)} %param.9) | copy-start | bytes 52
  7.2 5.0 %copy-start.3 = (f32[4,64]{1,0:T(4,128)S(1)}, f32[4,64]{1,0:T(4,128)}, u32[]{:S(2)}) copy-start(f32[4,64]{1,0:T(4,128)} %param.8) | copy-start | bytes 3076
  7.2 181.7 %copy-start.2 = (f32[64,64]{1,0:T(8,128)S(1)}, f32[64,64]{1,0:T(8,128)}, u32[]{:S(2)}) copy-start(f32[64,64]{1,0:T(8,128)} %param.7) | copy-start | bytes 49156
  7.2 181.5 %all-reduce.3.cloned.1.call-start = ((), (), s32[]{:S(2)}) async-start(), calls=%async_computation | async-start | bytes 1048576 | tf_op jit(solution)/shard_map/psum | solution.py:62
  11.9 417.6 %all-reduce.5.cloned.1.call-start = ((), (), s32[]{:S(2)}) async-start(), calls=%async_computation.1 | async-start | bytes 393216 | tf_op jit(solution)/shard_map/psum | solution.py:75
  210.0 0.8 copy-start.1
Sparse Core Ops, SparseCore 0:
  12.0 176.7 all-reduce.2
  212.9 216.5 all-reduce.4
where the time goes:
time: 438 us
  waiting for transfers between devices  285 us (65%)
  blocking collectives  104 us (24%)
  matrix products  28.7 us (7%)
  between operations  14.3 us (3%)
  local copies, waits for them, and re-layouts  4.52 us (1%)
    psum x1, waiting for transfers between devices, local(): raw_sums = lax.psum(local_sums, 'item')  176 us
    psum x1, waiting for transfers between devices, local(): item_total, shared_total = lax.psum((item_part, shared_part), 'stu')  109 us
    psum x1, blocking collectives, local(): item_total, shared_total = lax.psum((item_part, shared_part), 'stu')  104 us
  transfers between devices with their start and end apart: 2, of which 2 were waited for; matrix products, arithmetic and copies ran while one was open for 1% of the time, Pallas kernels for 0%

commit v1 on v0

--- a/solution.py
+++ b/solution.py
@@ -59,7 +59,7 @@
     counts = blocks[0]
     full_owners = owner_table(counts, row_total, 128)
     local_sums = jnp.dot(attempts, item_factor, preferred_element_type=jnp.float32)
-    raw_sums = lax.psum(local_sums, "item")
+    raw_sums = jnp.sum(lax.all_gather(local_sums, "item"), axis=0)
     target = scaled_target(raw_sums, full_owners, 128, student_weights, core_factor)
     orthogonal = polar_factor(target, full_owners, 128, lambda summand: summand)
     crossed = student_cross(orthogonal, raw_sums, full_owners, 128)

time: 438 us -> 399 us (0.911)
  waiting for transfers between devices: 285 us -> 234 us
  local copies, waits for them, and re-layouts: 4.52 us -> 11.6 us
    psum x1 -> x0, waiting for transfers between devices: 176 us -> none  [local(): raw_sums = lax.psum(local_sums, 'item')]
    all_gather x0 -> x1, waiting for transfers between devices: none -> 128 us  [local(): raw_sums = jnp.sum(lax.all_gather(local_sums, 'item'), axis=0)]
    unnamed x12 -> x10, local copies, waits for them, and re-layouts: 4.33 us -> 11.6 us
where the time goes in v1:
time: 399 us
  waiting for transfers between devices  234 us (59%)
  blocking collectives  107 us (27%)
  matrix products  28.4 us (7%)
  between operations  14.2 us (4%)
  local copies, waits for them, and re-layouts  11.6 us (3%)
    all_gather x1, waiting for transfers between devices, local(): raw_sums = jnp.sum(lax.all_gather(local_sums, 'item'), axis=0)  128 us
    psum x1, blocking collectives, local(): item_total, shared_total = lax.psum((item_part, shared_part), 'stu')  107 us
    psum x1, waiting for transfers between devices, local(): item_total, shared_total = lax.psum((item_part, shared_part), 'stu')  106 us
    unnamed x10, local copies, waits for them, and re-layouts  11.6 us
  transfers between devices with their start and end apart: 2, of which 2 were waited for; matrix products, arithmetic and copies ran while one was open for 1% of the time, Pallas kernels for 0%

profile of v1, /device:TPU:2, one launch (start us, length us, event | category | flops | bytes accessed | tf_op | source)
XLA Modules:
  0.0 398.5 jit_solution(12385973965452160905)
XLA Ops:
  7.2 0.0 copy-start
  7.2 0.0 copy-start.3
  7.2 0.0 copy-start.2
  7.2 0.0 all-gather.3.cloned.1.call-start
  7.2 1.8 copy-done
  9.1 2.8 fusion.72
  11.9 0.0 all-gather.3.cloned.1.call-update
  11.9 0.0 all-reduce.2.cloned.1.call-start
  11.9 0.0 copy-done.3
  11.9 0.2 reduce-window.4
  12.2 0.1 compare_and_fusion
  12.2 0.0 copy-done.2
  12.3 0.2 fusion.73
  12.4 127.9 %all-gather.3.cloned.1.call-done = f32[32768,64]{0,1:T(8,128)} async-done(((f32[2048,64]{0,1:T(8,128)}), f32[32768,64]{0,1:T(8,128)}) %all-gather.3.cloned.1.call-update) | async-done | bytes 8388624 | tf_op jit(solution)/shard_map/all_gather | solution.py:62
  140.4 8.1 %copy.43 = f32[8,8,16,2048]{3,2,1,0:T(8,128)S(1)} copy(f32[8,8,16,2048]{3,1,2,0:T(8,128)} %bitcast.113) | data formatting | bytes 16777216
  148.5 0.0 copy-start.1
  148.5 1.7 bitcast_reduce_fusion
  150.2 0.0 copy-done.1
  150.2 0.7 fusion.9
  151.0 0.9 fusion.74
  151.9 0.8 multiply_reduce_fusion.2
  152.7 0.1 convolution_bitcast_fusion.1
  152.8 0.5 fusion.38
  153.3 1.1 fusion.27
  154.4 0.9 fusion.75
  155.4 0.6 fusion.6
  156.0 0.7 fusion.62
  156.6 1.1 fusion.24
  157.7 0.9 fusion.76
  158.7 0.6 fusion.5
  159.3 0.5 fusion.59
  159.8 1.1 fusion.21
  160.9 0.9 fusion.77
  161.8 0.6 fusion.4
  162.4 0.5 fusion.56
  162.9 1.1 fusion.18
  164.0 0.9 fusion.78
  164.9 0.6 fusion.3
  165.5 0.5 fusion.53
  166.0 1.1 fusion.15
  167.1 0.9 fusion.79
  168.0 0.6 fusion.2
  168.7 0.5 fusion.50
  169.1 1.3 fusion.12
  170.4 1.7 fusion.7
  172.2 0.6 fusion.1
  172.8 1.3 convolution_bitcast_fusion
  174.1 0.0 all-reduce.2.cloned.1.call-update
  174.2 1.7 multiply_reduce_fusion.1
  175.8 107.2 %psum.15 = f32[64,64]{1,0:T(8,128)} all-reduce(f32[64,64]{1,0:T(8,128)S(1)} %bitcast.115), channel_id=1, replica_groups=mesh['stu'=32,'item'=16] {'stu'}, use_global_device_ids=true, to_apply=%region_4.5 | all-reduce | flops 4096 | bytes 32768 | tf_op jit(solution)/shard_map/psum | solution.py:75
  283.0 0.7 multiply_reduce_fusion
  283.7 106.4 %all-reduce.2.cloned.1.call-done = f32[768,64]{0,1:T(8,128)} async-done(((f32[768,64]{0,1:T(8,128)}), f32[768,64]{0,1:T(8,128)}) %all-reduce.2.cloned.1.call-update) | async-done | bytes 196624 | tf_op jit(solution)/shard_map/psum | solution.py:75
  390.1 1.6 copy.87
  (6 shorter events, 0.0 us)
Async XLA Ops:
  7.2 1.9 copy-start
  7.2 4.8 %copy-start.3 = (s32[1,4]{1,0:T(1,128)S(1)}, s32[1,4]{1,0:T(1,128)}, u32[]{:S(2)}) copy-start(s32[1,4]{1,0:T(1,128)} %param.9) | copy-start | bytes 52
  7.2 5.1 %copy-start.2 = (f32[4,64]{1,0:T(4,128)S(1)}, f32[4,64]{1,0:T(4,128)}, u32[]{:S(2)}) copy-start(f32[4,64]{1,0:T(4,128)} %param.8) | copy-start | bytes 3076
  7.2 133.2 %all-gather.3.cloned.1.call-start = ((), (), s32[]{:S(2)}) async-start(), calls=%async_computation.1 | async-start | bytes 8912896 | tf_op jit(solution)/shard_map/all_gather | solution.py:62
  11.9 378.2 %all-reduce.2.cloned.1.call-start = ((), (), s32[]{:S(2)}) async-start(), calls=%async_computation | async-start | bytes 393216 | tf_op jit(solution)/shard_map/psum | solution.py:75
  148.5 1.7 copy-start.1
Sparse Core Ops, SparseCore 0:
  12.0 128.3 all-gather.2
  174.3 215.7 all-reduce.1
